TPU v7x, 256 devices: a whole 4x4x8 slice. The times are simulated.
256 devices in a mesh: ctx: 8 (over y, core), exp: 32 (over x, z).
Axes of the slice: x: 4, y: 4, z: 8, core: 2. Of those that a mesh axis runs over, the one named last changes fastest.
Arguments:
- tokens: bfloat16 [32, 1024, 2048], P('exp', 'ctx'), may hold values from -6 to 6
- input_gain: float32 [2048], replicated, may hold values from 0.1 to 1.9
- mixer_weight: bfloat16 [2048, 6144], P(None, 'ctx'), may hold values from -0.125 to 0.125
- rate_weight: bfloat16 [2048, 8, 4], P(None, 'ctx'), may hold values from -3 to 3
- conv_kernel: float32 [4, 8, 512], P(None, 'ctx'), may hold values from -3 to 3
- decay_scale: float32 [16], P('ctx'), may hold values from 0 to 0.05
- decay_bias: float32 [16], P('ctx'), may hold values from -3 to 3
- value_gain: float32 [128], replicated, may hold values from 0.1 to 1.9
- output_weight: bfloat16 [2048, 2048], P('ctx'), may hold values from -0.125 to 0.125
- start_state: float32 [16, 128, 128], P('ctx'), may hold values from -0.8 to 0.8
- post_gain: float32 [2048], replicated, may hold values from 0.1 to 1.9
- expert_gateup: bfloat16 [32, 2048, 1024], P('exp'), may hold values from -0.125 to 0.125
- expert_down: bfloat16 [32, 512, 2048], P('exp'), may hold values from -0.25 to 0.25
- route_ids: int32 [32, 1024, 4], P('exp', 'ctx'), may hold values from 0 to 31, all different within a row; in each aligned block of 128 rows (0 to 127, 128 to 255, ..., all dimensions but the last counted through in order) at most 20 rows name the same one
- route_weights: float32 [32, 1024, 4], P('exp', 'ctx'), may hold values from 0.05 to 0.5
Outputs:
- layer_out: float32 [32, 1024, 2048], P('exp', 'ctx')
- segment_states: float32 [32, 16, 128, 128], P('exp', 'ctx')
Inputs may be any that keep to these rules, and one draw needn't show every extreme that they name: `route_ids`: each token names 4 different experts. Within the 128 rows of one device (aligned blocks) no expert is named by more than 20 rows, a bound that some block reaches.
All inputs are finite; a program needn't handle non-finite values.
Results may differ from a plain program's by a relative error of at most 0.012.
Values may be sent and summed in bfloat16 or wider, within the bound.
No kernel may reach another device: no remote copies, remote signals or barrier semaphores. Data moves between devices by JAX's collectives and lax.ppermute only.
A program may use at most 128 MiB of HBM per device.

v0:
```python
import jax
import jax.numpy as jnp
from jax import lax
from jax.sharding import PartitionSpec as P

DK = 128
DV = 128
FFE = 512
KCONV = 4
HK = 8
HV = 16
BLOCK = 64
ROUTES = 4
EPSILON = 1e-06
highest = lax.Precision.HIGHEST


def passed_along(block, axis, distance):
    devices = range(lax.axis_size(axis))
    route = [(i - distance, i) for i in devices if i - distance in devices]
    return lax.ppermute(block, axis, route)


def rms_scale(values, scaling):
    widened = values.astype(jnp.float32)
    return (
        widened * lax.rsqrt(jnp.mean(widened * widened, axis=-1, keepdims=True) + EPSILON) * scaling
    )


def unit_rows(values):
    return values * lax.rsqrt(jnp.sum(values * values, axis=-1, keepdims=True) + EPSILON)


def lower_solve(strict_lower, right_side):
    result = right_side - jnp.einsum(
        "...ij,...jk->...ik", strict_lower, right_side, precision=highest
    )
    powered = strict_lower
    for _ in range((strict_lower.shape[-1] - 1).bit_length() - 1):
        powered = jnp.einsum("...ij,...jk->...ik", powered, powered, precision=highest)
        result = result + jnp.einsum("...ij,...jk->...ik", powered, result, precision=highest)
    return result


def short_conv(pre_conv, tail_rows, kernel):
    padded = jnp.concatenate([tail_rows, pre_conv], axis=0).astype(jnp.float32)
    length = pre_conv.shape[0]
    summed = jnp.zeros(pre_conv.shape, jnp.float32)
    for offset in range(kernel.shape[0]):
        summed = summed + kernel[offset] * padded[offset : offset + length]
    return jax.nn.silu(summed)


def to_blocks(array):
    moved = jnp.moveaxis(array, 1, 0)
    return moved.reshape((moved.shape[0], moved.shape[1] // BLOCK, BLOCK) + moved.shape[2:])


def head_inputs(activated, rate_rows, decay_scale, decay_bias):
    length = activated.shape[0]
    per_group = HV // HK
    head_count = activated.shape[1] * per_group
    queries = jnp.repeat(unit_rows(activated[..., :DK]) * DK ** (-0.5), per_group, axis=1)
    key_rows = jnp.repeat(unit_rows(activated[..., DK : 2 * DK]), per_group, axis=1)
    values = activated[..., 2 * DK :].reshape(length, head_count, DV)
    betas = jax.nn.sigmoid(rate_rows[..., :per_group].astype(jnp.float32)).reshape(
        length, head_count
    )
    decay_input = rate_rows[..., per_group:].astype(jnp.float32).reshape(length, head_count)
    decays = -decay_scale * jax.nn.softplus(decay_input + decay_bias)
    return (
        to_blocks(queries),
        to_blocks(key_rows),
        to_blocks(values),
        to_blocks(betas),
        to_blocks(decays),
    )


def block_terms(queries, key_rows, values, betas, decays):
    cumulative = jnp.cumsum(decays, axis=-1)
    row_index = jnp.arange(BLOCK)[:, None]
    col_index = jnp.arange(BLOCK)[None, :]
    decay_gaps = cumulative[..., :, None] - cumulative[..., None, :]
    causal = jnp.exp(jnp.where(row_index >= col_index, decay_gaps, -1e30))
    strict = jnp.where(row_index > col_index, causal, 0.0)
    key_gram = jnp.einsum("hncd,hnmd->hncm", key_rows, key_rows, precision=highest)
    strict_lower = betas[..., :, None] * key_gram * strict
    grown = jnp.exp(cumulative)[..., None]
    right_side = jnp.concatenate(
        [betas[..., None] * key_rows * grown, betas[..., None] * values], axis=-1
    )
    solved = lower_solve(strict_lower, right_side)
    wide_keys = solved[..., :DK]
    new_values = solved[..., DK:]
    scores = jnp.einsum("hncd,hnmd->hncm", queries, key_rows, precision=highest) * causal
    readers = queries * grown - jnp.einsum("hncm,hnmd->hncd", scores, wide_keys, precision=highest)
    local_out = jnp.einsum("hncm,hnme->hnce", scores, new_values, precision=highest)
    last_sum = cumulative[..., -1:]
    faded_keys = key_rows * jnp.exp(last_sum - cumulative)[..., None]
    identity = jnp.eye(DK, dtype=jnp.float32)
    transfer = jnp.exp(last_sum)[..., None] * identity - jnp.einsum(
        "hncd,hnce->hnde", faded_keys, wide_keys, precision=highest
    )
    inject = jnp.einsum("hncd,hnce->hnde", faded_keys, new_values, precision=highest)
    return (readers, local_out, transfer, inject)


def apply_state(readers, state):
    return jnp.einsum("hcd,hde->hce", readers, state, precision=highest)


def advance(transfer, state):
    return jnp.einsum("hde,hef->hdf", transfer, state, precision=highest)


def gate_norm(mixer_out, gate_part, value_gain):
    normed = (
        mixer_out
        * lax.rsqrt(jnp.mean(mixer_out * mixer_out, axis=-1, keepdims=True) + EPSILON)
        * value_gain
    )
    gated = normed * jax.nn.silu(gate_part.astype(jnp.float32))
    return gated.reshape(mixer_out.shape[0], -1).astype(jnp.bfloat16)


def body(
    tokens,
    input_gain,
    mixer_weight,
    rate_weight,
    conv_kernel,
    decay_scale,
    decay_bias,
    value_gain,
    output_weight,
    start_state,
    post_gain,
    expert_gateup,
    expert_down,
    route_ids,
    route_weights,
):
    own_rows = tokens[0]
    tok_rows = own_rows.shape[0]
    model_width = own_rows.shape[1]
    conv_width = 2 * DK + HV // HK * DV
    normed = rms_scale(own_rows, input_gain).astype(jnp.bfloat16)
    segment = lax.all_gather(normed, "ctx", axis=0, tiled=True)
    seg_rows = segment.shape[0]
    groups = rate_weight.shape[1]
    projected = (
        jnp.dot(segment, mixer_weight, preferred_element_type=jnp.float32)
        .astype(jnp.bfloat16)
        .reshape(seg_rows, groups, -1)
    )
    rate_rows = (
        jnp.dot(segment, rate_weight.reshape(model_width, -1), preferred_element_type=jnp.float32)
        .astype(jnp.bfloat16)
        .reshape(seg_rows, groups, -1)
    )
    pre_conv = projected[..., :conv_width]
    tail_rows = passed_along(pre_conv[seg_rows - (KCONV - 1) :], "exp", 1)
    activated = short_conv(pre_conv, tail_rows, conv_kernel)
    queries, key_rows, values, betas, decays = head_inputs(
        activated, rate_rows, decay_scale, decay_bias
    )
    readers, local_out, transfer, inject = block_terms(queries, key_rows, values, betas, decays)
    stacked = tuple(
        (jnp.moveaxis(member, 1, 0) for member in (readers, local_out, transfer, inject))
    )
    heads_here = readers.shape[0]
    zero_state = jnp.zeros((heads_here, DK, DV), jnp.float32)
    identity = jnp.broadcast_to(jnp.eye(DK, dtype=jnp.float32), (heads_here, DK, DK))

    def summary_step(carried, block_parts):
        partial_state, product = carried
        return (
            (
                advance(block_parts[2], partial_state) + block_parts[3],
                advance(block_parts[2], product),
            ),
            None,
        )

    (seg_inject, seg_transfer), _ = lax.scan(summary_step, (zero_state, identity), stacked)
    first_device = lax.axis_index("exp") == 0

    def relay_step(counter, arriving):
        passed = passed_along(advance(seg_transfer, arriving) + seg_inject, "exp", 1)
        return jnp.where(first_device, start_state, passed)

    incoming = lax.fori_loop(
        0, lax.axis_size("exp") - 1, relay_step, jnp.where(first_device, start_state, zero_state)
    )

    def second_step(carried, block_parts):
        out_rows = apply_state(block_parts[0], carried) + block_parts[1]
        return (advance(block_parts[2], carried) + block_parts[3], out_rows)

    final_state, outputs = lax.scan(second_step, incoming, stacked)
    mixer_out = jnp.moveaxis(outputs, 0, 1).reshape(heads_here, seg_rows, DV).transpose(1, 0, 2)
    gate_part = projected[..., conv_width:].reshape(seg_rows, heads_here, DV)
    gated = gate_norm(mixer_out, gate_part, value_gain)
    mixed = lax.psum_scatter(
        jnp.dot(gated, output_weight, preferred_element_type=jnp.float32),
        "ctx",
        scatter_dimension=0,
        tiled=True,
    )
    hidden_state = own_rows.astype(jnp.float32) + mixed
    post = rms_scale(hidden_state, post_gain).astype(jnp.bfloat16)
    expert_count = lax.axis_size("exp")
    capacity = 5 * tok_rows * ROUTES // (4 * expert_count)
    id_list = route_ids[0].reshape(-1)
    onehot = (id_list[:, None] == jnp.arange(expert_count, dtype=jnp.int32)[None, :]).astype(
        jnp.int32
    )
    slots = jnp.sum((jnp.cumsum(onehot, axis=0) - onehot) * onehot, axis=1)
    destination = id_list * capacity + slots
    token_index = jnp.arange(tok_rows * ROUTES, dtype=jnp.int32) // ROUTES
    source_row = jnp.zeros(expert_count * capacity, jnp.int32).at[destination].set(token_index)
    filled = (
        jnp.zeros(expert_count * capacity, jnp.bfloat16)
        .at[destination]
        .set(jnp.ones(tok_rows * ROUTES, jnp.bfloat16))
    )
    outgoing = (post[source_row] * filled[:, None]).reshape(expert_count, capacity, model_width)
    arrived = lax.all_to_all(outgoing, "exp", split_axis=0, concat_axis=0, tiled=True)
    flat_rows = arrived.reshape(-1, model_width)
    gate_up = jnp.dot(flat_rows, expert_gateup[0], preferred_element_type=jnp.float32)
    expert_hidden = (jax.nn.silu(gate_up[:, :FFE]) * gate_up[:, FFE:]).astype(jnp.bfloat16)
    expert_out = jnp.dot(expert_hidden, expert_down[0], preferred_element_type=jnp.float32).astype(
        jnp.bfloat16
    )
    returned = lax.all_to_all(
        expert_out.reshape(arrived.shape), "exp", split_axis=0, concat_axis=0, tiled=True
    )
    picked = returned.reshape(expert_count * capacity, model_width)[destination].reshape(
        tok_rows, ROUTES, model_width
    )
    routed = jnp.sum(route_weights[0][..., None] * picked.astype(jnp.float32), axis=1)
    layer_out = hidden_state + routed
    return (layer_out[None], final_state[None])


def solution(mesh):
    in_specs = (
        P("exp", "ctx", None),
        P(),
        P(None, "ctx"),
        P(None, "ctx", None),
        P(None, "ctx", None),
        P("ctx"),
        P("ctx"),
        P(),
        P("ctx", None),
        P("ctx", None, None),
        P(),
        P("exp", None, None),
        P("exp", None, None),
        P("exp", "ctx", None),
        P("exp", "ctx", None),
    )
    out_specs = (P("exp", "ctx", None), P("exp", "ctx", None, None))
    return jax.shard_map(body, mesh=mesh, in_specs=in_specs, out_specs=out_specs, check_vma=False)
```

profile of v0, /device:TPU:8, one launch (start us, length us, event | category | flops | bytes accessed | tf_op | source)
XLA Modules:
  0.0 751.0 jit_solution(10715073160736058607)
XLA Ops:
  13.3 34.1 %all-gather.2.cloned.1.call-done = bf16[1024,2048]{1,0:T(8,128)(2,1)} async-done(((bf16[128,2048]{1,0:T(8,128)(2,1)}), bf16[1024,2048]{1,0:T(8,128)(2,1)}) %all-gather.2.cloned.1.call-update) | async-done | bytes 4194320 | tf_op jit(solution)/shard_map/all_gather | solution.py:150
  47.4 5.7 fusion.31
  112.1 24.2 %while.37 = (s32[]{:T(128)}, f32[2,128,128]{2,1,0:T(8,128)S(1)}, f32[2,128,128]{2,1,0:T(8,128)S(1)}, f32[16,2,128,128]{3,2,1,0:T(8,128)S(1)}, f32[16,2,128,128]{3,2,1,0:T(8,128)}, /*index=5*/s32[]{:T(128)}, s32[]{:T(128)}) while((s32[]{:T(128)}, f32[2,128,128]{2,1,0:T(8,128)S(1)}, f32[2,128,128]{2,1,0:T(8,128)S(1)}, ...), condition=%wide.region_4.5_spmd.clone, body=%wide.region_3.4_spmd.clone.sunk | while | flops 100728832 | bytes 1442907 | solution.py:187
  136.3 267.1 %while.35 = (s32[]{:T(128)}, f32[2,128,128]{2,1,0:T(8,128)S(1)}, pred[]{:T(512)}, f32[2,128,128]{2,1,0:T(8,128)S(1)}, f32[2,128,128]{2,1,0:T(8,128)S(1)}, /*index=5*/f32[2,128,128]{2,1,0:T(8,128)S(1)}, s32[]{:T(128)}) while((s32[]{:T(128)}, f32[2,128,128]{2,1,0:T(8,128)S(1)}, pred[]{:T(512)}, f32[2,128,128]{2,1,0:T(8,128)S(1)}, ...), condition=%wide.region_6.7_spmd, body=%wide.region_5.6_spmd.sunk | while | flops 50397184 | bytes 1441910 | solution.py:194
  179.2 5.6 collective-permute-start
  188.5 6.1 collective-permute-start
  198.1 5.7 collective-permute-start
  214.5 5.6 collective-permute-start
  222.9 5.6 collective-permute-start
  231.4 5.6 collective-permute-start
  239.7 5.8 collective-permute-start
  249.3 6.2 collective-permute-start
  274.9 5.6 collective-permute-start
  283.3 5.6 collective-permute-start
  291.7 5.7 collective-permute-start
  300.2 6.7 collective-permute-start
  309.7 5.9 collective-permute-start
  318.4 6.5 collective-permute-start
  327.8 6.9 collective-permute-start
  338.7 6.7 collective-permute-start
  348.5 6.3 collective-permute-start
  357.7 6.8 collective-permute-start
  367.3 6.2 collective-permute-start
  376.3 6.3 collective-permute-start
  385.4 6.1 collective-permute-start
  394.4 6.5 collective-permute-start
  403.4 47.4 %while.36 = (s32[]{:T(128)}, f32[2,128,128]{2,1,0:T(8,128)S(1)}, f32[16,2,64,128]{3,2,0,1:T(8,128)}, f32[16,2,128,128]{3,2,1,0:T(8,128)S(1)}, f32[16,2,128,128]{...) while((s32[]{:T(128)}, f32[2,128,128]{2,1,0:T(8,128)S(1)}, ...), condition=%wide.region_9.10_spmd, body=%wide.region_8.9_spmd.sunk | while | flops 75546624 | bytes 1116245 | solution.py:202
  468.7 65.3 %reduce-scatter.2.cloned.1.call-done = f32[128,2048]{1,0:T(8,128)} async-done(((f32[1024,2048]{1,0:T(8,128)}), f32[128,2048]{1,0:T(8,128)}) %reduce-scatter.2.cloned.1.call-update) | async-done | bytes 1048592 | tf_op jit(solution)/shard_map/reduce_scatter | solution.py:206
  547.2 83.5 %all_to_all.10 = bf16[32,20,2048]{2,1,0:T(8,128)(2,1)} all-to-all(bf16[32,20,2048]{2,1,0:T(8,128)(2,1)S(1)} %broadcast_multiply_fusion), channel_id=1, replica_groups=mesh['ctx'=8,'exp'=32] {'exp'}, dimensions={0} | all-to-all | bytes 5242880 | tf_op jit(solution)/shard_map/all_to_all | solution.py:230
  643.1 7.2 all-to-all-start.1
  650.4 74.7 %all-to-all-done.1 = bf16[32,20,2048]{2,1,0:T(8,128)(2,1)} async-done(((bf16[32,20,2048]{2,1,0:T(8,128)(2,1)}), bf16[32,20,2048]{2,1,0:T(8,128)(2,1)}, u32[]{:S(2)}, u32[]{:S(2)}) %all-to-all-start.1) | async-done | bytes 2621472 | tf_op jit(solution)/shard_map/all_to_all | solution.py:237
  736.9 5.6 multiply_reduce_fusion
  (382 shorter events, 323.2 us)
Async XLA Ops:
  7.2 40.2 %all-gather.2.cloned.1.call-start = ((), (), s32[]{:S(2)}) async-start(), calls=%async_computation.3 | async-start | bytes 4718592 | tf_op jit(solution)/shard_map/all_gather | solution.py:150
  10.7 523.3 %reduce-scatter.2.cloned.1.call-start = ((), (), s32[]{:S(2)}) async-start(), calls=%async_computation.4 | async-start | bytes 9437184 | tf_op jit(solution)/shard_map/reduce_scatter | solution.py:206
  53.3 11.6 %collective-permute-start.1 = (bf16[3,1,512]{2,0,1:T(4,128)(2,1)S(1)}, bf16[3,1,512]{2,0,1:T(4,128)(2,1)S(1)}, u32[]{:S(2)}, u32[]{:S(2)}) collective-permute-start(bf16[3,1,512]{2,0,1:T(4,128)(2,1)S(1)} %slice.99), channel_id=1, source_target_pairs={{0,1},{1,2},{2,3},{3,4},{4,5},{5,6},{6,7},{7,8},{8,9},{9,10},{10,1... | collective-permute-start | bytes 9224 | tf_op jit(solution)/shard_map/ppermute | solution.py:21
  143.2 6.9 collective-permute-start
  150.4 6.9 collective-permute-start
  172.0 6.9 collective-permute-start
  179.2 9.0 %collective-permute-start = (f32[2,128,128]{2,1,0:T(8,128)S(1)}, f32[2,128,128]{2,1,0:T(8,128)S(1)}, u32[]{:S(2)}, u32[]{:S(2)}) collective-permute-start(f32[2,128,128]{2,1,0:T(8,128)S(1)} %convolution_add_fusion.10), channel_id=1, source_target_pairs={{0,1},{1,2},{2,3},{3,4},{4,5},{5,6},{6,7},{7,8},{8,9},{9,10},{10,1... | collective-permute-start | bytes 393224 | tf_op jit(solution)/shard_map/while/body/eval_jaxpr/ppermute | solution.py:21
  188.5 9.3 %collective-permute-start = (f32[2,128,128]{2,1,0:T(8,128)S(1)}, f32[2,128,128]{2,1,0:T(8,128)S(1)}, u32[]{:S(2)}, u32[]{:S(2)}) collective-permute-start(f32[2,128,128]{2,1,0:T(8,128)S(1)} %convolution_add_fusion.10), channel_id=1, source_target_pairs={{0,1},{1,2},{2,3},{3,4},{4,5},{5,6},{6,7},{7,8},{8,9},{9,10},{10,1... | collective-permute-start | bytes 393224 | tf_op jit(solution)/shard_map/while/body/eval_jaxpr/ppermute | solution.py:21
  198.1 8.2 %collective-permute-start = (f32[2,128,128]{2,1,0:T(8,128)S(1)}, f32[2,128,128]{2,1,0:T(8,128)S(1)}, u32[]{:S(2)}, u32[]{:S(2)}) collective-permute-start(f32[2,128,128]{2,1,0:T(8,128)S(1)} %convolution_add_fusion.10), channel_id=1, source_target_pairs={{0,1},{1,2},{2,3},{3,4},{4,5},{5,6},{6,7},{7,8},{8,9},{9,10},{10,1... | collective-permute-start | bytes 393224 | tf_op jit(solution)/shard_map/while/body/eval_jaxpr/ppermute | solution.py:21
  206.6 7.6 %collective-permute-start = (f32[2,128,128]{2,1,0:T(8,128)S(1)}, f32[2,128,128]{2,1,0:T(8,128)S(1)}, u32[]{:S(2)}, u32[]{:S(2)}) collective-permute-start(f32[2,128,128]{2,1,0:T(8,128)S(1)} %convolution_add_fusion.10), channel_id=1, source_target_pairs={{0,1},{1,2},{2,3},{3,4},{4,5},{5,6},{6,7},{7,8},{8,9},{9,10},{10,1... | collective-permute-start | bytes 393224 | tf_op jit(solution)/shard_map/while/body/eval_jaxpr/ppermute | solution.py:21
  214.5 8.1 %collective-permute-start = (f32[2,128,128]{2,1,0:T(8,128)S(1)}, f32[2,128,128]{2,1,0:T(8,128)S(1)}, u32[]{:S(2)}, u32[]{:S(2)}) collective-permute-start(f32[2,128,128]{2,1,0:T(8,128)S(1)} %convolution_add_fusion.10), channel_id=1, source_target_pairs={{0,1},{1,2},{2,3},{3,4},{4,5},{5,6},{6,7},{7,8},{8,9},{9,10},{10,1... | collective-permute-start | bytes 393224 | tf_op jit(solution)/shard_map/while/body/eval_jaxpr/ppermute | solution.py:21
  222.9 8.1 %collective-permute-start = (f32[2,128,128]{2,1,0:T(8,128)S(1)}, f32[2,128,128]{2,1,0:T(8,128)S(1)}, u32[]{:S(2)}, u32[]{:S(2)}) collective-permute-start(f32[2,128,128]{2,1,0:T(8,128)S(1)} %convolution_add_fusion.10), channel_id=1, source_target_pairs={{0,1},{1,2},{2,3},{3,4},{4,5},{5,6},{6,7},{7,8},{8,9},{9,10},{10,1... | collective-permute-start | bytes 393224 | tf_op jit(solution)/shard_map/while/body/eval_jaxpr/ppermute | solution.py:21
  231.4 8.1 %collective-permute-start = (f32[2,128,128]{2,1,0:T(8,128)S(1)}, f32[2,128,128]{2,1,0:T(8,128)S(1)}, u32[]{:S(2)}, u32[]{:S(2)}) collective-permute-start(f32[2,128,128]{2,1,0:T(8,128)S(1)} %convolution_add_fusion.10), channel_id=1, source_target_pairs={{0,1},{1,2},{2,3},{3,4},{4,5},{5,6},{6,7},{7,8},{8,9},{9,10},{10,1... | collective-permute-start | bytes 393224 | tf_op jit(solution)/shard_map/while/body/eval_jaxpr/ppermute | solution.py:21
  239.7 9.3 %collective-permute-start = (f32[2,128,128]{2,1,0:T(8,128)S(1)}, f32[2,128,128]{2,1,0:T(8,128)S(1)}, u32[]{:S(2)}, u32[]{:S(2)}) collective-permute-start(f32[2,128,128]{2,1,0:T(8,128)S(1)} %convolution_add_fusion.10), channel_id=1, source_target_pairs={{0,1},{1,2},{2,3},{3,4},{4,5},{5,6},{6,7},{7,8},{8,9},{9,10},{10,1... | collective-permute-start | bytes 393224 | tf_op jit(solution)/shard_map/while/body/eval_jaxpr/ppermute | solution.py:21
  249.3 9.2 %collective-permute-start = (f32[2,128,128]{2,1,0:T(8,128)S(1)}, f32[2,128,128]{2,1,0:T(8,128)S(1)}, u32[]{:S(2)}, u32[]{:S(2)}) collective-permute-start(f32[2,128,128]{2,1,0:T(8,128)S(1)} %convolution_add_fusion.10), channel_id=1, source_target_pairs={{0,1},{1,2},{2,3},{3,4},{4,5},{5,6},{6,7},{7,8},{8,9},{9,10},{10,1... | collective-permute-start | bytes 393224 | tf_op jit(solution)/shard_map/while/body/eval_jaxpr/ppermute | solution.py:21
  258.9 7.7 %collective-permute-start = (f32[2,128,128]{2,1,0:T(8,128)S(1)}, f32[2,128,128]{2,1,0:T(8,128)S(1)}, u32[]{:S(2)}, u32[]{:S(2)}) collective-permute-start(f32[2,128,128]{2,1,0:T(8,128)S(1)} %convolution_add_fusion.10), channel_id=1, source_target_pairs={{0,1},{1,2},{2,3},{3,4},{4,5},{5,6},{6,7},{7,8},{8,9},{9,10},{10,1... | collective-permute-start | bytes 393224 | tf_op jit(solution)/shard_map/while/body/eval_jaxpr/ppermute | solution.py:21
  266.9 7.6 %collective-permute-start = (f32[2,128,128]{2,1,0:T(8,128)S(1)}, f32[2,128,128]{2,1,0:T(8,128)S(1)}, u32[]{:S(2)}, u32[]{:S(2)}) collective-permute-start(f32[2,128,128]{2,1,0:T(8,128)S(1)} %convolution_add_fusion.10), channel_id=1, source_target_pairs={{0,1},{1,2},{2,3},{3,4},{4,5},{5,6},{6,7},{7,8},{8,9},{9,10},{10,1... | collective-permute-start | bytes 393224 | tf_op jit(solution)/shard_map/while/body/eval_jaxpr/ppermute | solution.py:21
  274.9 8.1 %collective-permute-start = (f32[2,128,128]{2,1,0:T(8,128)S(1)}, f32[2,128,128]{2,1,0:T(8,128)S(1)}, u32[]{:S(2)}, u32[]{:S(2)}) collective-permute-start(f32[2,128,128]{2,1,0:T(8,128)S(1)} %convolution_add_fusion.10), channel_id=1, source_target_pairs={{0,1},{1,2},{2,3},{3,4},{4,5},{5,6},{6,7},{7,8},{8,9},{9,10},{10,1... | collective-permute-start | bytes 393224 | tf_op jit(solution)/shard_map/while/body/eval_jaxpr/ppermute | solution.py:21
  283.3 8.1 %collective-permute-start = (f32[2,128,128]{2,1,0:T(8,128)S(1)}, f32[2,128,128]{2,1,0:T(8,128)S(1)}, u32[]{:S(2)}, u32[]{:S(2)}) collective-permute-start(f32[2,128,128]{2,1,0:T(8,128)S(1)} %convolution_add_fusion.10), channel_id=1, source_target_pairs={{0,1},{1,2},{2,3},{3,4},{4,5},{5,6},{6,7},{7,8},{8,9},{9,10},{10,1... | collective-permute-start | bytes 393224 | tf_op jit(solution)/shard_map/while/body/eval_jaxpr/ppermute | solution.py:21
  291.7 8.2 %collective-permute-start = (f32[2,128,128]{2,1,0:T(8,128)S(1)}, f32[2,128,128]{2,1,0:T(8,128)S(1)}, u32[]{:S(2)}, u32[]{:S(2)}) collective-permute-start(f32[2,128,128]{2,1,0:T(8,128)S(1)} %convolution_add_fusion.10), channel_id=1, source_target_pairs={{0,1},{1,2},{2,3},{3,4},{4,5},{5,6},{6,7},{7,8},{8,9},{9,10},{10,1... | collective-permute-start | bytes 393224 | tf_op jit(solution)/shard_map/while/body/eval_jaxpr/ppermute | solution.py:21
  300.2 9.2 %collective-permute-start = (f32[2,128,128]{2,1,0:T(8,128)S(1)}, f32[2,128,128]{2,1,0:T(8,128)S(1)}, u32[]{:S(2)}, u32[]{:S(2)}) collective-permute-start(f32[2,128,128]{2,1,0:T(8,128)S(1)} %convolution_add_fusion.10), channel_id=1, source_target_pairs={{0,1},{1,2},{2,3},{3,4},{4,5},{5,6},{6,7},{7,8},{8,9},{9,10},{10,1... | collective-permute-start | bytes 393224 | tf_op jit(solution)/shard_map/while/body/eval_jaxpr/ppermute | solution.py:21
  309.7 8.4 %collective-permute-start = (f32[2,128,128]{2,1,0:T(8,128)S(1)}, f32[2,128,128]{2,1,0:T(8,128)S(1)}, u32[]{:S(2)}, u32[]{:S(2)}) collective-permute-start(f32[2,128,128]{2,1,0:T(8,128)S(1)} %convolution_add_fusion.10), channel_id=1, source_target_pairs={{0,1},{1,2},{2,3},{3,4},{4,5},{5,6},{6,7},{7,8},{8,9},{9,10},{10,1... | collective-permute-start | bytes 393224 | tf_op jit(solution)/shard_map/while/body/eval_jaxpr/ppermute | solution.py:21
  318.4 9.0 %collective-permute-start = (f32[2,128,128]{2,1,0:T(8,128)S(1)}, f32[2,128,128]{2,1,0:T(8,128)S(1)}, u32[]{:S(2)}, u32[]{:S(2)}) collective-permute-start(f32[2,128,128]{2,1,0:T(8,128)S(1)} %convolution_add_fusion.10), channel_id=1, source_target_pairs={{0,1},{1,2},{2,3},{3,4},{4,5},{5,6},{6,7},{7,8},{8,9},{9,10},{10,1... | collective-permute-start | bytes 393224 | tf_op jit(solution)/shard_map/while/body/eval_jaxpr/ppermute | solution.py:21
  327.8 10.7 %collective-permute-start = (f32[2,128,128]{2,1,0:T(8,128)S(1)}, f32[2,128,128]{2,1,0:T(8,128)S(1)}, u32[]{:S(2)}, u32[]{:S(2)}) collective-permute-start(f32[2,128,128]{2,1,0:T(8,128)S(1)} %convolution_add_fusion.10), channel_id=1, source_target_pairs={{0,1},{1,2},{2,3},{3,4},{4,5},{5,6},{6,7},{7,8},{8,9},{9,10},{10,1... | collective-permute-start | bytes 393224 | tf_op jit(solution)/shard_map/while/body/eval_jaxpr/ppermute | solution.py:21
  338.7 9.5 %collective-permute-start = (f32[2,128,128]{2,1,0:T(8,128)S(1)}, f32[2,128,128]{2,1,0:T(8,128)S(1)}, u32[]{:S(2)}, u32[]{:S(2)}) collective-permute-start(f32[2,128,128]{2,1,0:T(8,128)S(1)} %convolution_add_fusion.10), channel_id=1, source_target_pairs={{0,1},{1,2},{2,3},{3,4},{4,5},{5,6},{6,7},{7,8},{8,9},{9,10},{10,1... | collective-permute-start | bytes 393224 | tf_op jit(solution)/shard_map/while/body/eval_jaxpr/ppermute | solution.py:21
  348.5 8.8 %collective-permute-start = (f32[2,128,128]{2,1,0:T(8,128)S(1)}, f32[2,128,128]{2,1,0:T(8,128)S(1)}, u32[]{:S(2)}, u32[]{:S(2)}) collective-permute-start(f32[2,128,128]{2,1,0:T(8,128)S(1)} %convolution_add_fusion.10), channel_id=1, source_target_pairs={{0,1},{1,2},{2,3},{3,4},{4,5},{5,6},{6,7},{7,8},{8,9},{9,10},{10,1... | collective-permute-start | bytes 393224 | tf_op jit(solution)/shard_map/while/body/eval_jaxpr/ppermute | solution.py:21
  357.7 9.3 %collective-permute-start = (f32[2,128,128]{2,1,0:T(8,128)S(1)}, f32[2,128,128]{2,1,0:T(8,128)S(1)}, u32[]{:S(2)}, u32[]{:S(2)}) collective-permute-start(f32[2,128,128]{2,1,0:T(8,128)S(1)} %convolution_add_fusion.10), channel_id=1, source_target_pairs={{0,1},{1,2},{2,3},{3,4},{4,5},{5,6},{6,7},{7,8},{8,9},{9,10},{10,1... | collective-permute-start | bytes 393224 | tf_op jit(solution)/shard_map/while/body/eval_jaxpr/ppermute | solution.py:21
  367.3 8.7 %collective-permute-start = (f32[2,128,128]{2,1,0:T(8,128)S(1)}, f32[2,128,128]{2,1,0:T(8,128)S(1)}, u32[]{:S(2)}, u32[]{:S(2)}) collective-permute-start(f32[2,128,128]{2,1,0:T(8,128)S(1)} %convolution_add_fusion.10), channel_id=1, source_target_pairs={{0,1},{1,2},{2,3},{3,4},{4,5},{5,6},{6,7},{7,8},{8,9},{9,10},{10,1... | collective-permute-start | bytes 393224 | tf_op jit(solution)/shard_map/while/body/eval_jaxpr/ppermute | solution.py:21
  376.3 8.8 %collective-permute-start = (f32[2,128,128]{2,1,0:T(8,128)S(1)}, f32[2,128,128]{2,1,0:T(8,128)S(1)}, u32[]{:S(2)}, u32[]{:S(2)}) collective-permute-start(f32[2,128,128]{2,1,0:T(8,128)S(1)} %convolution_add_fusion.10), channel_id=1, source_target_pairs={{0,1},{1,2},{2,3},{3,4},{4,5},{5,6},{6,7},{7,8},{8,9},{9,10},{10,1... | collective-permute-start | bytes 393224 | tf_op jit(solution)/shard_map/while/body/eval_jaxpr/ppermute | solution.py:21
  385.4 8.6 %collective-permute-start = (f32[2,128,128]{2,1,0:T(8,128)S(1)}, f32[2,128,128]{2,1,0:T(8,128)S(1)}, u32[]{:S(2)}, u32[]{:S(2)}) collective-permute-start(f32[2,128,128]{2,1,0:T(8,128)S(1)} %convolution_add_fusion.10), channel_id=1, source_target_pairs={{0,1},{1,2},{2,3},{3,4},{4,5},{5,6},{6,7},{7,8},{8,9},{9,10},{10,1... | collective-permute-start | bytes 393224 | tf_op jit(solution)/shard_map/while/body/eval_jaxpr/ppermute | solution.py:21
  394.4 9.0 %collective-permute-start = (f32[2,128,128]{2,1,0:T(8,128)S(1)}, f32[2,128,128]{2,1,0:T(8,128)S(1)}, u32[]{:S(2)}, u32[]{:S(2)}) collective-permute-start(f32[2,128,128]{2,1,0:T(8,128)S(1)} %convolution_add_fusion.10), channel_id=1, source_target_pairs={{0,1},{1,2},{2,3},{3,4},{4,5},{5,6},{6,7},{7,8},{8,9},{9,10},{10,1... | collective-permute-start | bytes 393224 | tf_op jit(solution)/shard_map/while/body/eval_jaxpr/ppermute | solution.py:21
  643.1 82.0 %all-to-all-start.1 = ((bf16[32,20,2048]{2,1,0:T(8,128)(2,1)}), bf16[32,20,2048]{2,1,0:T(8,128)(2,1)}, u32[]{:S(2)}, u32[]{:S(2)}) async-start(bf16[32,20,2048]{2,1,0:T(8,128)(2,1)} %reshape.235), calls=%async_computation.2 | async-start | bytes 6291456 | tf_op jit(solution)/shard_map/all_to_all | solution.py:237
  (38 other events, 407.6 us)
Sparse Core Ops, SparseCore 0:
  10.8 36.5 all-gather.1
  459.4 74.5 reduce-scatter.1
where the time goes:
time: 757 us; the launch traced here: 751 us
  waiting for transfers between devices  257 us (34%)
  starting transfers between devices  186 us (25%)
  matrix products  130 us (17%)
  blocking collectives  83.5 us (11%)
  local copies, waits for them, and re-layouts  49.8 us (7%)
  other arithmetic  27.2 us (4%)
  between operations  15.3 us (2%)
    ppermute x32, starting transfers between devices, passed_along(): return lax.ppermute(block, axis, route)  179 us
    all_to_all x1, blocking collectives, body(): lax.all_to_all(outgoing, 'exp', split_axis=0, concat_axis=0, tiled=True)  83.5 us
    ppermute x32, waiting for transfers between devices, passed_along(): return lax.ppermute(block, axis, route)  82.5 us
    all_to_all x1, waiting for transfers between devices, body(): lax.all_to_all(expert_out.reshape(arrived.shape), 'exp', split_axis=0, co...  74.7 us
    reduce_scatter x1, waiting for transfers between devices, body(): lax.psum_scatter(jnp.dot(gated, output_weight, preferred_element_type=jnp...  65.3 us
    dot_general x79, matrix products, advance(): return jnp.einsum('hde,hef->hdf', transfer, state, precision=highest)  50 us
    all_gather x1, waiting for transfers between devices, body(): segment = lax.all_gather(normed, 'ctx', axis=0, tiled=True)  34.1 us
    dot_general x16, matrix products, apply_state(): return jnp.einsum('hcd,hde->hce', readers, state, precision=highest)  28 us
  transfers between devices with their start and end apart: 35, of which 34 were waited for; matrix products, arithmetic and copies ran while one was open for 3% of the time, Pallas kernels for 0%

commit v1 on v0

--- a/solution.py
+++ b/solution.py
@@ -147,7 +147,13 @@
     model_width = own_rows.shape[1]
     conv_width = 2 * DK + HV // HK * DV
     normed = rms_scale(own_rows, input_gain).astype(jnp.bfloat16)
-    segment = lax.all_gather(normed, "ctx", axis=0, tiled=True)
+    keep_up_the_frames = lambda base_x, which_axis: jnp.concatenate(
+        lax.all_to_all(
+            jnp.stack([base_x for _ in range(lax.axis_size(which_axis))], 0), which_axis, 0, 0
+        ),
+        axis=0,
+    )
+    segment = keep_up_the_frames(normed, which_axis="ctx")
     seg_rows = segment.shape[0]
     groups = rate_weight.shape[1]
     projected = (

time: 757 us -> 777 us (1.026)
  waiting for transfers between devices: 257 us -> 268 us
    all_to_all x0 -> x1, waiting for transfers between devices: none -> 46.4 us  [body(): lax.all_to_all(jnp.stack([base_x for _ in range(lax.axis_size(which_axis)...]
    all_gather x1 -> x0, waiting for transfers between devices: 34.1 us -> none  [body(): segment = lax.all_gather(normed, 'ctx', axis=0, tiled=True)]
where the time goes in v1:
time: 777 us; the launch traced here: 771 us
  waiting for transfers between devices  268 us (34%)
  starting transfers between devices  191 us (25%)
  matrix products  132 us (17%)
  blocking collectives  83.4 us (11%)
  local copies, waits for them, and re-layouts  52.2 us (7%)
  other arithmetic  25.8 us (3%)
  between operations  15.2 us (2%)
    ppermute x32, starting transfers between devices, passed_along(): return lax.ppermute(block, axis, route)  177 us
    all_to_all x1, blocking collectives, body(): lax.all_to_all(outgoing, 'exp', split_axis=0, concat_axis=0, tiled=True)  83.4 us
    ppermute x32, waiting for transfers between devices, passed_along(): return lax.ppermute(block, axis, route)  82.4 us
    all_to_all x1, waiting for transfers between devices, body(): lax.all_to_all(expert_out.reshape(arrived.shape), 'exp', split_axis=0, co...  74.7 us
    reduce_scatter x1, waiting for transfers between devices, body(): lax.psum_scatter(jnp.dot(gated, output_weight, preferred_element_type=jnp...  64.9 us
    dot_general x79, matrix products, advance(): return jnp.einsum('hde,hef->hdf', transfer, state, precision=highest)  50 us
    all_to_all x1, waiting for transfers between devices, body(): lax.all_to_all(jnp.stack([base_x for _ in range(lax.axis_size(which_axis)...  46.4 us
    dot_general x16, matrix products, apply_state(): return jnp.einsum('hcd,hde->hce', readers, state, precision=highest)  27.8 us
  transfers between devices with their start and end apart: 35, of which 34 were waited for; matrix products, arithmetic and copies ran while one was open for 3% of the time, Pallas kernels for 0%

profile of v1, /device:TPU:8, one launch (start us, length us, event | category | flops | bytes accessed | tf_op | source)
XLA Modules:
  0.0 770.6 jit_solution(766820020567078583)
XLA Ops:
  12.3 6.7 all-to-all-start
  21.0 46.4 %all-to-all-done = bf16[8,128,2048]{2,1,0:T(8,128)(2,1)} async-done(((bf16[8,128,2048]{2,1,0:T(8,128)(2,1)}), bf16[8,128,2048]{2,1,0:T(8,128)(2,1)}, u32[]{:S(2)}, u32[]{:S(2)}) %all-to-all-start) | async-done | bytes 4194336 | tf_op jit(solution)/shard_map/all_to_all | solution.py:151
  67.4 5.6 fusion.31
  132.8 24.2 %while.37 = (s32[]{:T(128)}, f32[2,128,128]{2,1,0:T(8,128)S(1)}, f32[2,128,128]{2,1,0:T(8,128)S(1)}, f32[16,2,128,128]{3,2,1,0:T(8,128)S(1)}, f32[16,2,128,128]{3,2,1,0:T(8,128)}, /*index=5*/s32[]{:T(128)}, s32[]{:T(128)}) while((s32[]{:T(128)}, f32[2,128,128]{2,1,0:T(8,128)S(1)}, f32[2,128,128]{2,1,0:T(8,128)S(1)}, ...), condition=%wide.region_4.5_spmd.clone, body=%wide.region_3.4_spmd.clone.sunk | while | flops 100728832 | bytes 1442907 | solution.py:193
  157.0 266.8 %while.35 = (s32[]{:T(128)}, f32[2,128,128]{2,1,0:T(8,128)S(1)}, pred[]{:T(512)}, f32[2,128,128]{2,1,0:T(8,128)S(1)}, f32[2,128,128]{2,1,0:T(8,128)S(1)}, /*index=5*/f32[2,128,128]{2,1,0:T(8,128)S(1)}, s32[]{:T(128)}) while((s32[]{:T(128)}, f32[2,128,128]{2,1,0:T(8,128)S(1)}, pred[]{:T(512)}, f32[2,128,128]{2,1,0:T(8,128)S(1)}, ...), condition=%wide.region_6.7_spmd, body=%wide.region_5.6_spmd.sunk | while | flops 50397184 | bytes 1441910 | solution.py:200
  201.5 5.9 collective-permute-start
  211.2 5.9 collective-permute-start
  228.1 5.6 collective-permute-start
  236.5 5.6 collective-permute-start
  244.9 5.6 collective-permute-start
  262.6 6.1 collective-permute-start
  272.2 5.8 collective-permute-start
  288.7 5.6 collective-permute-start
  297.1 5.6 collective-permute-start
  305.5 5.6 collective-permute-start
  313.9 5.6 collective-permute-start
  322.3 5.6 collective-permute-start
  339.0 6.3 collective-permute-start
  348.3 6.9 collective-permute-start
  359.3 6.4 collective-permute-start
  368.8 6.5 collective-permute-start
  378.1 6.7 collective-permute-start
  387.6 6.2 collective-permute-start
  396.6 6.3 collective-permute-start
  405.7 6.2 collective-permute-start
  414.8 6.5 collective-permute-start
  423.8 47.2 %while.36 = (s32[]{:T(128)}, f32[2,128,128]{2,1,0:T(8,128)S(1)}, f32[16,2,64,128]{3,2,0,1:T(8,128)}, f32[16,2,128,128]{3,2,1,0:T(8,128)S(1)}, f32[16,2,128,128]{...) while((s32[]{:T(128)}, f32[2,128,128]{2,1,0:T(8,128)S(1)}, ...), condition=%wide.region_9.10_spmd, body=%wide.region_8.9_spmd.sunk | while | flops 75546624 | bytes 1116245 | solution.py:208
  488.9 64.9 %reduce-scatter.2.cloned.1.call-done = f32[128,2048]{1,0:T(8,128)} async-done(((f32[1024,2048]{1,0:T(8,128)}), f32[128,2048]{1,0:T(8,128)}) %reduce-scatter.2.cloned.1.call-update) | async-done | bytes 1048592 | tf_op jit(solution)/shard_map/reduce_scatter | solution.py:212
  566.9 83.4 %all_to_all.15 = bf16[32,20,2048]{2,1,0:T(8,128)(2,1)} all-to-all(bf16[32,20,2048]{2,1,0:T(8,128)(2,1)S(1)} %broadcast_multiply_fusion), channel_id=1, replica_groups=mesh['ctx'=8,'exp'=32] {'exp'}, dimensions={0} | all-to-all | bytes 5242880 | tf_op jit(solution)/shard_map/all_to_all | solution.py:236
  662.7 7.2 all-to-all-start.2
  670.1 74.7 %all-to-all-done.2 = bf16[32,20,2048]{2,1,0:T(8,128)(2,1)} async-done(((bf16[32,20,2048]{2,1,0:T(8,128)(2,1)}), bf16[32,20,2048]{2,1,0:T(8,128)(2,1)}, u32[]{:S(2)}, u32[]{:S(2)}) %all-to-all-start.2) | async-done | bytes 2621472 | tf_op jit(solution)/shard_map/all_to_all | solution.py:243
  756.5 5.6 multiply_reduce_fusion
  (378 shorter events, 332.2 us)
Async XLA Ops:
  12.3 55.1 %all-to-all-start = ((bf16[8,128,2048]{2,1,0:T(8,128)(2,1)}), bf16[8,128,2048]{2,1,0:T(8,128)(2,1)}, u32[]{:S(2)}, u32[]{:S(2)}) async-start(bf16[8,128,2048]{2,1,0:T(8,128)(2,1)} %stack.5), calls=%async_computation | async-start | bytes 8388608 | tf_op jit(solution)/shard_map/all_to_all | solution.py:151
  19.1 534.7 %reduce-scatter.2.cloned.1.call-start = ((), (), s32[]{:S(2)}) async-start(), calls=%async_computation.4 | async-start | bytes 9437184 | tf_op jit(solution)/shard_map/reduce_scatter | solution.py:212
  73.2 12.4 %collective-permute-start.1 = (bf16[3,1,512]{2,0,1:T(4,128)(2,1)S(1)}, bf16[3,1,512]{2,0,1:T(4,128)(2,1)S(1)}, u32[]{:S(2)}, u32[]{:S(2)}) collective-permute-start(bf16[3,1,512]{2,0,1:T(4,128)(2,1)S(1)} %slice.99), channel_id=1, source_target_pairs={{0,1},{1,2},{2,3},{3,4},{4,5},{5,6},{6,7},{7,8},{8,9},{9,10},{10,1... | collective-permute-start | bytes 9224 | tf_op jit(solution)/shard_map/ppermute | solution.py:21
  163.9 6.9 collective-permute-start
  171.1 7.0 collective-permute-start
  192.7 8.5 %collective-permute-start = (f32[2,128,128]{2,1,0:T(8,128)S(1)}, f32[2,128,128]{2,1,0:T(8,128)S(1)}, u32[]{:S(2)}, u32[]{:S(2)}) collective-permute-start(f32[2,128,128]{2,1,0:T(8,128)S(1)} %convolution_add_fusion.10), channel_id=1, source_target_pairs={{0,1},{1,2},{2,3},{3,4},{4,5},{5,6},{6,7},{7,8},{8,9},{9,10},{10,1... | collective-permute-start | bytes 393224 | tf_op jit(solution)/shard_map/while/body/eval_jaxpr/ppermute | solution.py:21
  201.5 9.3 %collective-permute-start = (f32[2,128,128]{2,1,0:T(8,128)S(1)}, f32[2,128,128]{2,1,0:T(8,128)S(1)}, u32[]{:S(2)}, u32[]{:S(2)}) collective-permute-start(f32[2,128,128]{2,1,0:T(8,128)S(1)} %convolution_add_fusion.10), channel_id=1, source_target_pairs={{0,1},{1,2},{2,3},{3,4},{4,5},{5,6},{6,7},{7,8},{8,9},{9,10},{10,1... | collective-permute-start | bytes 393224 | tf_op jit(solution)/shard_map/while/body/eval_jaxpr/ppermute | solution.py:21
  211.2 8.4 %collective-permute-start = (f32[2,128,128]{2,1,0:T(8,128)S(1)}, f32[2,128,128]{2,1,0:T(8,128)S(1)}, u32[]{:S(2)}, u32[]{:S(2)}) collective-permute-start(f32[2,128,128]{2,1,0:T(8,128)S(1)} %convolution_add_fusion.10), channel_id=1, source_target_pairs={{0,1},{1,2},{2,3},{3,4},{4,5},{5,6},{6,7},{7,8},{8,9},{9,10},{10,1... | collective-permute-start | bytes 393224 | tf_op jit(solution)/shard_map/while/body/eval_jaxpr/ppermute | solution.py:21
  219.9 7.9 %collective-permute-start = (f32[2,128,128]{2,1,0:T(8,128)S(1)}, f32[2,128,128]{2,1,0:T(8,128)S(1)}, u32[]{:S(2)}, u32[]{:S(2)}) collective-permute-start(f32[2,128,128]{2,1,0:T(8,128)S(1)} %convolution_add_fusion.10), channel_id=1, source_target_pairs={{0,1},{1,2},{2,3},{3,4},{4,5},{5,6},{6,7},{7,8},{8,9},{9,10},{10,1... | collective-permute-start | bytes 393224 | tf_op jit(solution)/shard_map/while/body/eval_jaxpr/ppermute | solution.py:21
  228.1 8.1 %collective-permute-start = (f32[2,128,128]{2,1,0:T(8,128)S(1)}, f32[2,128,128]{2,1,0:T(8,128)S(1)}, u32[]{:S(2)}, u32[]{:S(2)}) collective-permute-start(f32[2,128,128]{2,1,0:T(8,128)S(1)} %convolution_add_fusion.10), channel_id=1, source_target_pairs={{0,1},{1,2},{2,3},{3,4},{4,5},{5,6},{6,7},{7,8},{8,9},{9,10},{10,1... | collective-permute-start | bytes 393224 | tf_op jit(solution)/shard_map/while/body/eval_jaxpr/ppermute | solution.py:21
  236.5 8.1 %collective-permute-start = (f32[2,128,128]{2,1,0:T(8,128)S(1)}, f32[2,128,128]{2,1,0:T(8,128)S(1)}, u32[]{:S(2)}, u32[]{:S(2)}) collective-permute-start(f32[2,128,128]{2,1,0:T(8,128)S(1)} %convolution_add_fusion.10), channel_id=1, source_target_pairs={{0,1},{1,2},{2,3},{3,4},{4,5},{5,6},{6,7},{7,8},{8,9},{9,10},{10,1... | collective-permute-start | bytes 393224 | tf_op jit(solution)/shard_map/while/body/eval_jaxpr/ppermute | solution.py:21
  244.9 8.1 %collective-permute-start = (f32[2,128,128]{2,1,0:T(8,128)S(1)}, f32[2,128,128]{2,1,0:T(8,128)S(1)}, u32[]{:S(2)}, u32[]{:S(2)}) collective-permute-start(f32[2,128,128]{2,1,0:T(8,128)S(1)} %convolution_add_fusion.10), channel_id=1, source_target_pairs={{0,1},{1,2},{2,3},{3,4},{4,5},{5,6},{6,7},{7,8},{8,9},{9,10},{10,1... | collective-permute-start | bytes 393224 | tf_op jit(solution)/shard_map/while/body/eval_jaxpr/ppermute | solution.py:21
  253.3 9.0 %collective-permute-start = (f32[2,128,128]{2,1,0:T(8,128)S(1)}, f32[2,128,128]{2,1,0:T(8,128)S(1)}, u32[]{:S(2)}, u32[]{:S(2)}) collective-permute-start(f32[2,128,128]{2,1,0:T(8,128)S(1)} %convolution_add_fusion.10), channel_id=1, source_target_pairs={{0,1},{1,2},{2,3},{3,4},{4,5},{5,6},{6,7},{7,8},{8,9},{9,10},{10,1... | collective-permute-start | bytes 393224 | tf_op jit(solution)/shard_map/while/body/eval_jaxpr/ppermute | solution.py:21
  262.6 9.3 %collective-permute-start = (f32[2,128,128]{2,1,0:T(8,128)S(1)}, f32[2,128,128]{2,1,0:T(8,128)S(1)}, u32[]{:S(2)}, u32[]{:S(2)}) collective-permute-start(f32[2,128,128]{2,1,0:T(8,128)S(1)} %convolution_add_fusion.10), channel_id=1, source_target_pairs={{0,1},{1,2},{2,3},{3,4},{4,5},{5,6},{6,7},{7,8},{8,9},{9,10},{10,1... | collective-permute-start | bytes 393224 | tf_op jit(solution)/shard_map/while/body/eval_jaxpr/ppermute | solution.py:21
  272.2 8.3 %collective-permute-start = (f32[2,128,128]{2,1,0:T(8,128)S(1)}, f32[2,128,128]{2,1,0:T(8,128)S(1)}, u32[]{:S(2)}, u32[]{:S(2)}) collective-permute-start(f32[2,128,128]{2,1,0:T(8,128)S(1)} %convolution_add_fusion.10), channel_id=1, source_target_pairs={{0,1},{1,2},{2,3},{3,4},{4,5},{5,6},{6,7},{7,8},{8,9},{9,10},{10,1... | collective-permute-start | bytes 393224 | tf_op jit(solution)/shard_map/while/body/eval_jaxpr/ppermute | solution.py:21
  280.8 7.6 collective-permute-start
  288.7 8.1 %collective-permute-start = (f32[2,128,128]{2,1,0:T(8,128)S(1)}, f32[2,128,128]{2,1,0:T(8,128)S(1)}, u32[]{:S(2)}, u32[]{:S(2)}) collective-permute-start(f32[2,128,128]{2,1,0:T(8,128)S(1)} %convolution_add_fusion.10), channel_id=1, source_target_pairs={{0,1},{1,2},{2,3},{3,4},{4,5},{5,6},{6,7},{7,8},{8,9},{9,10},{10,1... | collective-permute-start | bytes 393224 | tf_op jit(solution)/shard_map/while/body/eval_jaxpr/ppermute | solution.py:21
  297.1 8.1 %collective-permute-start = (f32[2,128,128]{2,1,0:T(8,128)S(1)}, f32[2,128,128]{2,1,0:T(8,128)S(1)}, u32[]{:S(2)}, u32[]{:S(2)}) collective-permute-start(f32[2,128,128]{2,1,0:T(8,128)S(1)} %convolution_add_fusion.10), channel_id=1, source_target_pairs={{0,1},{1,2},{2,3},{3,4},{4,5},{5,6},{6,7},{7,8},{8,9},{9,10},{10,1... | collective-permute-start | bytes 393224 | tf_op jit(solution)/shard_map/while/body/eval_jaxpr/ppermute | solution.py:21
  305.5 8.1 %collective-permute-start = (f32[2,128,128]{2,1,0:T(8,128)S(1)}, f32[2,128,128]{2,1,0:T(8,128)S(1)}, u32[]{:S(2)}, u32[]{:S(2)}) collective-permute-start(f32[2,128,128]{2,1,0:T(8,128)S(1)} %convolution_add_fusion.10), channel_id=1, source_target_pairs={{0,1},{1,2},{2,3},{3,4},{4,5},{5,6},{6,7},{7,8},{8,9},{9,10},{10,1... | collective-permute-start | bytes 393224 | tf_op jit(solution)/shard_map/while/body/eval_jaxpr/ppermute | solution.py:21
  313.9 8.1 %collective-permute-start = (f32[2,128,128]{2,1,0:T(8,128)S(1)}, f32[2,128,128]{2,1,0:T(8,128)S(1)}, u32[]{:S(2)}, u32[]{:S(2)}) collective-permute-start(f32[2,128,128]{2,1,0:T(8,128)S(1)} %convolution_add_fusion.10), channel_id=1, source_target_pairs={{0,1},{1,2},{2,3},{3,4},{4,5},{5,6},{6,7},{7,8},{8,9},{9,10},{10,1... | collective-permute-start | bytes 393224 | tf_op jit(solution)/shard_map/while/body/eval_jaxpr/ppermute | solution.py:21
  322.3 8.1 %collective-permute-start = (f32[2,128,128]{2,1,0:T(8,128)S(1)}, f32[2,128,128]{2,1,0:T(8,128)S(1)}, u32[]{:S(2)}, u32[]{:S(2)}) collective-permute-start(f32[2,128,128]{2,1,0:T(8,128)S(1)} %convolution_add_fusion.10), channel_id=1, source_target_pairs={{0,1},{1,2},{2,3},{3,4},{4,5},{5,6},{6,7},{7,8},{8,9},{9,10},{10,1... | collective-permute-start | bytes 393224 | tf_op jit(solution)/shard_map/while/body/eval_jaxpr/ppermute | solution.py:21
  330.7 8.1 %collective-permute-start = (f32[2,128,128]{2,1,0:T(8,128)S(1)}, f32[2,128,128]{2,1,0:T(8,128)S(1)}, u32[]{:S(2)}, u32[]{:S(2)}) collective-permute-start(f32[2,128,128]{2,1,0:T(8,128)S(1)} %convolution_add_fusion.10), channel_id=1, source_target_pairs={{0,1},{1,2},{2,3},{3,4},{4,5},{5,6},{6,7},{7,8},{8,9},{9,10},{10,1... | collective-permute-start | bytes 393224 | tf_op jit(solution)/shard_map/while/body/eval_jaxpr/ppermute | solution.py:21
  339.0 8.9 %collective-permute-start = (f32[2,128,128]{2,1,0:T(8,128)S(1)}, f32[2,128,128]{2,1,0:T(8,128)S(1)}, u32[]{:S(2)}, u32[]{:S(2)}) collective-permute-start(f32[2,128,128]{2,1,0:T(8,128)S(1)} %convolution_add_fusion.10), channel_id=1, source_target_pairs={{0,1},{1,2},{2,3},{3,4},{4,5},{5,6},{6,7},{7,8},{8,9},{9,10},{10,1... | collective-permute-start | bytes 393224 | tf_op jit(solution)/shard_map/while/body/eval_jaxpr/ppermute | solution.py:21
  348.3 10.7 %collective-permute-start = (f32[2,128,128]{2,1,0:T(8,128)S(1)}, f32[2,128,128]{2,1,0:T(8,128)S(1)}, u32[]{:S(2)}, u32[]{:S(2)}) collective-permute-start(f32[2,128,128]{2,1,0:T(8,128)S(1)} %convolution_add_fusion.10), channel_id=1, source_target_pairs={{0,1},{1,2},{2,3},{3,4},{4,5},{5,6},{6,7},{7,8},{8,9},{9,10},{10,1... | collective-permute-start | bytes 393224 | tf_op jit(solution)/shard_map/while/body/eval_jaxpr/ppermute | solution.py:21
  359.3 9.2 %collective-permute-start = (f32[2,128,128]{2,1,0:T(8,128)S(1)}, f32[2,128,128]{2,1,0:T(8,128)S(1)}, u32[]{:S(2)}, u32[]{:S(2)}) collective-permute-start(f32[2,128,128]{2,1,0:T(8,128)S(1)} %convolution_add_fusion.10), channel_id=1, source_target_pairs={{0,1},{1,2},{2,3},{3,4},{4,5},{5,6},{6,7},{7,8},{8,9},{9,10},{10,1... | collective-permute-start | bytes 393224 | tf_op jit(solution)/shard_map/while/body/eval_jaxpr/ppermute | solution.py:21
  368.8 9.0 %collective-permute-start = (f32[2,128,128]{2,1,0:T(8,128)S(1)}, f32[2,128,128]{2,1,0:T(8,128)S(1)}, u32[]{:S(2)}, u32[]{:S(2)}) collective-permute-start(f32[2,128,128]{2,1,0:T(8,128)S(1)} %convolution_add_fusion.10), channel_id=1, source_target_pairs={{0,1},{1,2},{2,3},{3,4},{4,5},{5,6},{6,7},{7,8},{8,9},{9,10},{10,1... | collective-permute-start | bytes 393224 | tf_op jit(solution)/shard_map/while/body/eval_jaxpr/ppermute | solution.py:21
  378.1 9.2 %collective-permute-start = (f32[2,128,128]{2,1,0:T(8,128)S(1)}, f32[2,128,128]{2,1,0:T(8,128)S(1)}, u32[]{:S(2)}, u32[]{:S(2)}) collective-permute-start(f32[2,128,128]{2,1,0:T(8,128)S(1)} %convolution_add_fusion.10), channel_id=1, source_target_pairs={{0,1},{1,2},{2,3},{3,4},{4,5},{5,6},{6,7},{7,8},{8,9},{9,10},{10,1... | collective-permute-start | bytes 393224 | tf_op jit(solution)/shard_map/while/body/eval_jaxpr/ppermute | solution.py:21
  387.6 8.7 %collective-permute-start = (f32[2,128,128]{2,1,0:T(8,128)S(1)}, f32[2,128,128]{2,1,0:T(8,128)S(1)}, u32[]{:S(2)}, u32[]{:S(2)}) collective-permute-start(f32[2,128,128]{2,1,0:T(8,128)S(1)} %convolution_add_fusion.10), channel_id=1, source_target_pairs={{0,1},{1,2},{2,3},{3,4},{4,5},{5,6},{6,7},{7,8},{8,9},{9,10},{10,1... | collective-permute-start | bytes 393224 | tf_op jit(solution)/shard_map/while/body/eval_jaxpr/ppermute | solution.py:21
  396.6 8.8 %collective-permute-start = (f32[2,128,128]{2,1,0:T(8,128)S(1)}, f32[2,128,128]{2,1,0:T(8,128)S(1)}, u32[]{:S(2)}, u32[]{:S(2)}) collective-permute-start(f32[2,128,128]{2,1,0:T(8,128)S(1)} %convolution_add_fusion.10), channel_id=1, source_target_pairs={{0,1},{1,2},{2,3},{3,4},{4,5},{5,6},{6,7},{7,8},{8,9},{9,10},{10,1... | collective-permute-start | bytes 393224 | tf_op jit(solution)/shard_map/while/body/eval_jaxpr/ppermute | solution.py:21
  405.7 8.7 %collective-permute-start = (f32[2,128,128]{2,1,0:T(8,128)S(1)}, f32[2,128,128]{2,1,0:T(8,128)S(1)}, u32[]{:S(2)}, u32[]{:S(2)}) collective-permute-start(f32[2,128,128]{2,1,0:T(8,128)S(1)} %convolution_add_fusion.10), channel_id=1, source_target_pairs={{0,1},{1,2},{2,3},{3,4},{4,5},{5,6},{6,7},{7,8},{8,9},{9,10},{10,1... | collective-permute-start | bytes 393224 | tf_op jit(solution)/shard_map/while/body/eval_jaxpr/ppermute | solution.py:21
  414.8 9.0 %collective-permute-start = (f32[2,128,128]{2,1,0:T(8,128)S(1)}, f32[2,128,128]{2,1,0:T(8,128)S(1)}, u32[]{:S(2)}, u32[]{:S(2)}) collective-permute-start(f32[2,128,128]{2,1,0:T(8,128)S(1)} %convolution_add_fusion.10), channel_id=1, source_target_pairs={{0,1},{1,2},{2,3},{3,4},{4,5},{5,6},{6,7},{7,8},{8,9},{9,10},{10,1... | collective-permute-start | bytes 393224 | tf_op jit(solution)/shard_map/while/body/eval_jaxpr/ppermute | solution.py:21
  662.7 82.1 %all-to-all-start.2 = ((bf16[32,20,2048]{2,1,0:T(8,128)(2,1)}), bf16[32,20,2048]{2,1,0:T(8,128)(2,1)}, u32[]{:S(2)}, u32[]{:S(2)}) async-start(bf16[32,20,2048]{2,1,0:T(8,128)(2,1)} %reshape.253), calls=%async_computation.3 | async-start | bytes 6291456 | tf_op jit(solution)/shard_map/all_to_all | solution.py:243
  (36 other events, 386.2 us)
Sparse Core Ops, SparseCore 0:
  479.6 74.1 reduce-scatter.1
